TPU v7x, 128 devices: a whole 4x4x4 slice. The times are simulated.
128 devices in a mesh: grp: 16 (over x, y), hist: 8 (over z, core).
Axes of the slice: x: 4, y: 4, z: 4, core: 2. Of those that a mesh axis runs over, the one named last changes fastest.
Arguments:
- cand_tokens: bfloat16 [32768, 1024], P(('grp', 'hist')), may hold values from -6 to 6
- cand_user: int32 [32768], P('grp'), may hold values from 0 to 1
- hist_len: int32 [32], P('grp'), may hold values from 1 to 8192
- req_owner: int32 [16, 8, 16, 1], P('grp', 'hist'), may hold values from 0 to 15; in each aligned block of 16 rows (0 to 15, 16 to 31, ..., all dimensions but the last counted through in order) at most 2 rows name the same one
- req_slot: int32 [16, 8, 16], P('grp', 'hist'), may hold values from 0 to 15
- hist_embed: bfloat16 [256, 8, 128, 1024], P('grp', 'hist'), may hold values from -6 to 6
- w_query: bfloat16 [1024, 1024], replicated, may hold values from -0.1875 to 0.1875
- w_key: bfloat16 [1024, 1024], replicated, may hold values from -0.1875 to 0.1875
- w_value: bfloat16 [1024, 1024], replicated, may hold values from -0.1875 to 0.1875
- w_gate: bfloat16 [1024, 1024], replicated, may hold values from -0.1875 to 0.1875
- w_out: bfloat16 [1024, 1024], replicated, may hold values from -0.1875 to 0.1875
Outputs:
- ranked: bfloat16 [32768, 1024], P(('grp', 'hist'))
Inputs may be any that keep to these rules, and one draw needn't show every extreme that they name: `req_owner`: at most 2 of one device's 16 requests name the same owner, and in every draw some device sends exactly 2 to one owner.
All inputs are finite; a program needn't handle non-finite values.
Results may differ from a plain program's by a relative error of at most 0.0053.
Values may be sent and summed in bfloat16 or wider, within the bound.
A program may use at most 128 MiB of HBM per device.

v0:
```python
import math

import jax
import jax.numpy as jnp
from jax import lax
from jax.sharding import PartitionSpec as P

HEADS = 8
BPS = 8


NORM_EPS = 1e-06
LAYER_EPS = 1e-05


def rms_rows(block_rows):
    widened = block_rows.astype(jnp.float32)
    return widened * lax.rsqrt(jnp.mean(widened * widened, axis=-1, keepdims=True) + NORM_EPS)


def project(normed_rows, weight):
    return jax.nn.silu(jnp.dot(normed_rows, weight, preferred_element_type=jnp.float32))


def attend(queries, row_users, key_rows, values, key_user, key_valid):
    row_count = queries.shape[0]
    block_size = math.gcd(row_count, 512)
    head_size = key_rows.shape[1] // HEADS
    scale = 1.0 / math.sqrt(head_size)
    keys_heads = key_rows.reshape(-1, HEADS, head_size)
    values_heads = values.reshape(-1, HEADS, head_size)

    def one_block(block_index):
        first_row = block_index * block_size
        query_rows = lax.dynamic_slice_in_dim(queries, first_row, block_size, 0)
        query_rows = query_rows.reshape(block_size, HEADS, head_size)
        users_here = lax.dynamic_slice_in_dim(row_users, first_row, block_size, 0)
        allowed = (users_here[:, None] == key_user[None, :]) & key_valid[None, :]
        scores = (
            jnp.einsum("qhd,khd->hqk", query_rows, keys_heads, preferred_element_type=jnp.float32)
            * scale
        )
        weights = jnp.where(allowed[None], jax.nn.silu(scores), 0.0).astype(jnp.bfloat16)
        result = jnp.einsum(
            "hqk,khd->qhd", weights, values_heads, preferred_element_type=jnp.float32
        )
        return result.reshape(block_size, HEADS * head_size)

    blocks = lax.map(one_block, jnp.arange(row_count // block_size, dtype=jnp.int32))
    return blocks.reshape(row_count, HEADS * head_size)


def per_device(
    cand_tokens,
    cand_user,
    hist_len,
    req_owner,
    req_slot,
    hist_embed,
    w_query,
    w_key,
    w_value,
    w_gate,
    w_out,
):
    width = cand_tokens.shape[1]
    n_grp = lax.axis_size("grp")
    shard_id = lax.axis_index("hist")
    normed_tokens = rms_rows(cand_tokens).astype(jnp.bfloat16)
    queries = project(normed_tokens, w_query).astype(jnp.bfloat16)
    gate_act = project(normed_tokens, w_gate)
    group_queries = lax.all_gather(queries, "hist", axis=0, tiled=True)
    owners = req_owner[0, 0, :, 0]
    slots = req_slot[0, 0]
    req_count = owners.shape[0]
    capacity = 2 * ((req_count + n_grp - 1) // n_grp)
    request_order = jnp.arange(req_count, dtype=jnp.int32)
    before = (owners[None, :] == owners[:, None]) & (
        request_order[None, :] < request_order[:, None]
    )
    req_rank = jnp.sum(before.astype(jnp.int32), axis=1)
    target = owners * capacity + req_rank
    places = jnp.arange(n_grp * capacity, dtype=jnp.int32)
    chosen = places[:, None] == target[None, :]
    send_slots = jnp.sum(jnp.where(chosen, slots[None, :], 0), axis=1).reshape(n_grp, capacity)
    asked_slots = lax.all_to_all(
        send_slots, "grp", split_axis=0, concat_axis=0, tiled=True
    ).reshape(-1)
    own_cache = hist_embed[:, 0]
    block_len = own_cache.shape[1]
    cache_normed = rms_rows(own_cache).astype(jnp.bfloat16).reshape(-1, width)
    keys_owned = project(cache_normed, w_key).astype(jnp.bfloat16).reshape(own_cache.shape)
    values_owned = project(cache_normed, w_value).astype(jnp.bfloat16).reshape(own_cache.shape)
    picked_keys = jnp.take(keys_owned, asked_slots, axis=0).reshape(
        n_grp, capacity, block_len, width
    )
    picked_values = jnp.take(values_owned, asked_slots, axis=0).reshape(
        n_grp, capacity, block_len, width
    )
    back_keys, back_values = (
        lax.all_to_all(picked_keys, "grp", split_axis=0, concat_axis=0, tiled=True),
        lax.all_to_all(picked_values, "grp", split_axis=0, concat_axis=0, tiled=True),
    )
    key_rows = jnp.take(back_keys.reshape(-1, block_len, width), target, axis=0).reshape(-1, width)
    values = jnp.take(back_values.reshape(-1, block_len, width), target, axis=0).reshape(-1, width)
    action_order = jnp.arange(block_len, dtype=jnp.int32)
    key_user = jnp.repeat(request_order // BPS, block_len)
    positions = ((shard_id * BPS + request_order % BPS) * block_len)[:, None] + action_order[
        None, :
    ]
    key_valid = positions.reshape(-1) < jnp.take(hist_len, key_user, axis=0)
    attn = lax.psum_scatter(
        attend(group_queries, cand_user, key_rows, values, key_user, key_valid),
        "hist",
        scatter_dimension=0,
        tiled=True,
    )
    centred = attn - jnp.mean(attn, axis=-1, keepdims=True)
    attn_normed = centred * lax.rsqrt(
        jnp.mean(centred * centred, axis=-1, keepdims=True) + LAYER_EPS
    )
    gated = (attn_normed * gate_act).astype(jnp.bfloat16)
    mixed = cand_tokens.astype(jnp.float32) + jnp.dot(
        gated, w_out, preferred_element_type=jnp.float32
    )
    return mixed.astype(jnp.bfloat16)


def solution(mesh):
    placed = (
        P(("grp", "hist"), None),
        P("grp"),
        P("grp"),
        P("grp", "hist", None, None),
        P("grp", "hist", None),
        P("grp", "hist", None, None),
        P(),
        P(),
        P(),
        P(),
        P(),
    )
    return jax.shard_map(
        per_device, mesh=mesh, in_specs=placed, out_specs=P(("grp", "hist"), None), check_vma=False
    )
```

profile of v0, /device:TPU:1, one launch (start us, length us, event | category | flops | bytes accessed | tf_op | source)
XLA Modules:
  0.0 508.1 jit_solution(6928458724093586538)
XLA Ops:
  9.6 7.6 %all-to-all-start = ((s32[16,1,2]{2,1,0:T(1,128)}), s32[16,1,2]{2,1,0:T(1,128)S(1)}, u32[]{:S(2)}, u32[]{:S(2)}) async-start(s32[16,1,2]{2,1,0:T(1,128)} %bitcast.2), calls=%async_computation | async-start | bytes 16384 | tf_op jit(solution)/shard_map/all_to_all | solution.py:86
  17.2 3.2 multiply_reduce_fusion
  21.5 6.9 %multiply_convert_fusion.1 = bf16[2048,1024]{1,0:T(8,128)(2,1)} fusion(bf16[2048,1024]{1,0:T(8,128)(2,1)S(1)} %fusion.8, bf16[1024,1024]{1,0:T(8,128)(2,1)S(1)} %copy-done), kind=kOutput, calls=%fused_computation.22 | convolution fusion | flops 4305453056 | bytes 10485760 | tf_op jit(solution)/shard_map/dot_general | solution.py:22
  28.3 6.8 %multiply_convert_fusion = bf16[2048,1024]{1,0:T(8,128)(2,1)} fusion(bf16[2048,1024]{1,0:T(8,128)(2,1)S(1)} %fusion.8, bf16[1024,1024]{1,0:T(8,128)(2,1)S(1)} %copy-done.8), kind=kOutput, calls=%fused_computation.21 | convolution fusion | flops 4305453056 | bytes 10485760 | tf_op jit(solution)/shard_map/dot_general | solution.py:22
  36.5 7.2 %gather_fusion = bf16[32,128,1024]{2,1,0:T(8,128)(2,1)} fusion(bf16[16,128,1024]{2,1,0:T(8,128)(2,1)} %bitcast.84, s32[1024]{0:T(1024)S(1)} %pad_clamp_fusion.1), kind=kCustom, calls=%fused_computation.clone | custom fusion | bytes 16777344 | tf_op jit(solution)/shard_map/jit(_take)/gather | solution.py:94
  43.7 7.2 %gather_fusion.2 = bf16[32,128,1024]{2,1,0:T(8,128)(2,1)} fusion(bf16[16,128,1024]{2,1,0:T(8,128)(2,1)} %bitcast.83, s32[1024]{0:T(1024)S(1)} %pad_clamp_fusion.1), kind=kCustom, calls=%fused_computation.2.clone | custom fusion | bytes 16777344 | tf_op jit(solution)/shard_map/jit(_take)/gather | solution.py:97
  50.8 9.4 %broadcast_select_fusion = (bf16[32,128,1024]{2,1,0:T(8,128)(2,1)}, bf16[32,128,1024]{2,1,0:T(8,128)(2,1)S(1)}) fusion(bf16[32,128,1024]{2,1,0:T(8,128)(2,1)} %gather_fusion.2, pred[32]{0:T(512)(128)(4,1)S(1)} %compare_and_fusion.2, bf16[32,128,1024]{2,1,0:T(8,128)(2,1)} %gather_fusion), kind=kLoop, calls=%fused_computation.24 | loop fusion | flops 8388608 | bytes 33554464 | tf_op jit(solution)/shard_map/jit(_take)/select_n | solution.py:97
  60.2 99.4 %all_to_all.19 = bf16[16,2,128,1024]{3,2,1,0:T(8,128)(2,1)} all-to-all(bf16[16,2,128,1024]{3,2,1,0:T(8,128)(2,1)S(1)} %bitcast.80), channel_id=1, replica_groups=mesh['grp'=16,'hist'=8] {'grp'}, dimensions={0} | all-to-all | bytes 16777216 | tf_op jit(solution)/shard_map/all_to_all | solution.py:101
  159.7 6.3 %all-to-all-start.2 = ((bf16[16,2,128,1024]{3,2,1,0:T(8,128)(2,1)}), bf16[16,2,128,1024]{3,2,1,0:T(8,128)(2,1)}, u32[]{:S(2)}, u32[]{:S(2)}) async-start(bf16[16,2,128,1024]{3,2,1,0:T(8,128)(2,1)} %bitcast.79), calls=%async_computation.2 | async-start | bytes 16777216 | tf_op jit(solution)/shard_map/all_to_all | solution.py:102
  166.2 3.2 multiply_convert_fusion.3
  170.4 6.1 %gather_fusion.1 = bf16[16,128,1024]{2,1,0:T(8,128)(2,1)} fusion(bf16[32,128,1024]{2,1,0:T(8,128)(2,1)} %bitcast.82, s32[1024]{0:T(1024)S(1)} %pad_clamp_fusion), kind=kCustom, calls=%fused_computation.1.clone | custom fusion | bytes 8388672 | tf_op jit(solution)/shard_map/jit(_take)/gather | solution.py:104
  176.6 118.7 %all-to-all-done.2 = bf16[16,2,128,1024]{3,2,1,0:T(8,128)(2,1)} async-done(((bf16[16,2,128,1024]{3,2,1,0:T(8,128)(2,1)}), bf16[16,2,128,1024]{3,2,1,0:T(8,128)(2,1)}, u32[]{:S(2)}, u32[]{:S(2)}) %all-to-all-start.2) | async-done | bytes 8388640 | tf_op jit(solution)/shard_map/all_to_all | solution.py:102
  295.3 6.1 %gather_fusion.3 = bf16[16,128,1024]{2,1,0:T(8,128)(2,1)} fusion(bf16[32,128,1024]{2,1,0:T(8,128)(2,1)} %bitcast.10, s32[1024]{0:T(1024)S(1)} %pad_clamp_fusion), kind=kCustom, calls=%fused_computation.3.clone | custom fusion | bytes 8388672 | tf_op jit(solution)/shard_map/jit(_take)/gather | solution.py:105
  301.4 4.3 broadcast_select_fusion.2
  306.8 2.6 copy.27
  309.4 3.0 copy.39
  312.4 6.7 %copy.28 = bf16[2048,8,128]{0,2,1:T(8,128)(2,1)} copy(bf16[2048,8,128]{2,1,0:T(8,128)(2,1)} %bitcast.88) | data formatting | bytes 8388608
  319.1 112.7 %while.12 = (s32[]{:T(128)}, f32[4,512,1024]{2,1,0:T(8,128)}, s32[4]{0:T(128)S(1)}, s32[2048]{0:T(1024)}, bf16[2048,1024]{1,0:T(8,128)(2,1)}, /*index=5*/bf16[20...) while((s32[]{:T(128)}, f32[4,512,1024]{2,1,0:T(8,128)}, ...), condition=%wide.region_5.8_spmd.clone.clone, body=%wide.region_4.7_spmd.clone.clone.sunk | while | flops 4355813376 | bytes 26274776 | solution.py:49
  325.2 18.6 %fusion.47 = f32[8,512,128]{1,2,0:T(8,128)} fusion(bf16[2048,8,128]{0,2,1:T(8,128)(2,1)} %get-tuple-element.282, bf16[512,8,128]{0,2,1:T(8,128)(2,1)S(1)} %bitcast.81, bf16[2048,8,128]{2,0,1:T(8,128)(2,1)} %get-tuple-element.281, pred[512,2048]{1,0:T(8,128)(4,1)S(1)} %compare_and_fusion.4), kind=kOutput, calls=%fused_computation.7.clone.1 | convolution fusion | flops 4353687552 | bytes 12582912 | tf_op jit(solution)/shard_map/while/body/eval_jaxpr/hqk,khd->qhd/dot_general | solution.py:44
  343.8 1.9 copy.43
  345.7 1.6 constant_dynamic-update-slice_fusion.2
  353.4 18.6 %fusion.47 = f32[8,512,128]{1,2,0:T(8,128)} fusion(bf16[2048,8,128]{0,2,1:T(8,128)(2,1)} %get-tuple-element.282, bf16[512,8,128]{0,2,1:T(8,128)(2,1)S(1)} %bitcast.81, bf16[2048,8,128]{2,0,1:T(8,128)(2,1)} %get-tuple-element.281, pred[512,2048]{1,0:T(8,128)(4,1)S(1)} %compare_and_fusion.4), kind=kOutput, calls=%fused_computation.7.clone.1 | convolution fusion | flops 4353687552 | bytes 12582912 | tf_op jit(solution)/shard_map/while/body/eval_jaxpr/hqk,khd->qhd/dot_general | solution.py:44
  372.0 1.9 copy.43
  373.9 1.6 constant_dynamic-update-slice_fusion.2
  381.5 18.6 %fusion.47 = f32[8,512,128]{1,2,0:T(8,128)} fusion(bf16[2048,8,128]{0,2,1:T(8,128)(2,1)} %get-tuple-element.282, bf16[512,8,128]{0,2,1:T(8,128)(2,1)S(1)} %bitcast.81, bf16[2048,8,128]{2,0,1:T(8,128)(2,1)} %get-tuple-element.281, pred[512,2048]{1,0:T(8,128)(4,1)S(1)} %compare_and_fusion.4), kind=kOutput, calls=%fused_computation.7.clone.1 | convolution fusion | flops 4353687552 | bytes 12582912 | tf_op jit(solution)/shard_map/while/body/eval_jaxpr/hqk,khd->qhd/dot_general | solution.py:44
  400.1 1.9 copy.43
  402.0 1.6 constant_dynamic-update-slice_fusion.2
  409.7 18.6 %fusion.47 = f32[8,512,128]{1,2,0:T(8,128)} fusion(bf16[2048,8,128]{0,2,1:T(8,128)(2,1)} %get-tuple-element.282, bf16[512,8,128]{0,2,1:T(8,128)(2,1)S(1)} %bitcast.81, bf16[2048,8,128]{2,0,1:T(8,128)(2,1)} %get-tuple-element.281, pred[512,2048]{1,0:T(8,128)(4,1)S(1)} %compare_and_fusion.4), kind=kOutput, calls=%fused_computation.7.clone.1 | convolution fusion | flops 4353687552 | bytes 12582912 | tf_op jit(solution)/shard_map/while/body/eval_jaxpr/hqk,khd->qhd/dot_general | solution.py:44
  428.3 1.9 copy.43
  430.2 1.6 constant_dynamic-update-slice_fusion.2
  431.8 61.7 %reduce-scatter.2.cloned.1.call-done = f32[256,1024]{1,0:T(8,128)} async-done(((f32[2048,1024]{1,0:T(8,128)}), f32[256,1024]{1,0:T(8,128)}) %reduce-scatter.2.cloned.1.call-update) | async-done | bytes 1048592 | tf_op jit(solution)/shard_map/reduce_scatter | solution.py:112
  496.4 4.9 fusion.9
  (85 shorter events, 32.0 us)
Async XLA Ops:
  6.5 14.9 %copy-start = (bf16[1024,1024]{1,0:T(8,128)(2,1)S(1)}, bf16[1024,1024]{1,0:T(8,128)(2,1)}, u32[]{:S(2)}) copy-start(bf16[1024,1024]{1,0:T(8,128)(2,1)} %param.24) | copy-start | bytes 6291460
  9.6 25.5 %all-to-all-start = ((s32[16,1,2]{2,1,0:T(1,128)}), s32[16,1,2]{2,1,0:T(1,128)S(1)}, u32[]{:S(2)}, u32[]{:S(2)}) async-start(s32[16,1,2]{2,1,0:T(1,128)} %bitcast.2), calls=%async_computation | async-start | bytes 16384 | tf_op jit(solution)/shard_map/all_to_all | solution.py:86
  17.2 3.5 copy-start.2
  21.4 6.9 %copy-start.8 = (bf16[1024,1024]{1,0:T(8,128)(2,1)S(1)}, bf16[1024,1024]{1,0:T(8,128)(2,1)}, u32[]{:S(2)}) copy-start(bf16[1024,1024]{1,0:T(8,128)(2,1)} %param.25) | copy-start | bytes 6291460
  159.7 6.4 %copy-start.3 = (bf16[256,1024]{1,0:T(8,128)(2,1)S(1)}, bf16[256,1024]{1,0:T(8,128)(2,1)}, u32[]{:S(2)}) copy-start(bf16[256,1024]{1,0:T(8,128)(2,1)} %param.17) | copy-start | bytes 1572868
  159.7 135.6 %all-to-all-start.2 = ((bf16[16,2,128,1024]{3,2,1,0:T(8,128)(2,1)}), bf16[16,2,128,1024]{3,2,1,0:T(8,128)(2,1)}, u32[]{:S(2)}, u32[]{:S(2)}) async-start(bf16[16,2,128,1024]{3,2,1,0:T(8,128)(2,1)} %bitcast.79), calls=%async_computation.2 | async-start | bytes 16777216 | tf_op jit(solution)/shard_map/all_to_all | solution.py:102
  166.0 153.2 %all-gather.2.cloned.1.call-start = ((), (), s32[]{:S(2)}) async-start(), calls=%async_computation.4 | async-start | bytes 4718592 | tf_op jit(solution)/shard_map/all_gather | solution.py:72
  166.2 3.3 copy-start.6
  166.2 3.6 copy-start.5
  169.5 324.0 %reduce-scatter.2.cloned.1.call-start = ((), (), s32[]{:S(2)}) async-start(), calls=%async_computation.5 | async-start | bytes 9437184 | tf_op jit(solution)/shard_map/reduce_scatter | solution.py:112
  431.8 64.5 %copy-start.4 = (bf16[256,1024]{1,0:T(8,128)(2,1)S(1)}, bf16[256,1024]{1,0:T(8,128)(2,1)}, u32[]{:S(2)}) copy-start(bf16[256,1024]{1,0:T(8,128)(2,1)} %param.17) | copy-start | bytes 1572868
  431.8 64.6 %copy-start.7 = (f32[256]{0:T(256)S(1)}, f32[256]{0:T(256)}, u32[]{:S(2)}) copy-start(f32[256]{0:T(256)} %copy-done.6) | copy-start | bytes 3076
  496.3 5.0 copy-start.1
Sparse Core Ops, SparseCore 0:
  169.6 36.6 all-gather.1
  431.9 61.4 reduce-scatter.1
where the time goes:
time: 509 us; the launch traced here: 508 us
  waiting for transfers between devices  180 us (35%)
  blocking collectives  99.4 us (20%)
  matrix products  96.1 us (19%)
  local copies, waits for them, and re-layouts  69.5 us (14%)
  other arithmetic  32.1 us (6%)
  starting transfers between devices  14.2 us (3%)
  between operations  13.6 us (3%)
    all_to_all x1, waiting for transfers between devices, per_device(): lax.all_to_all(picked_values, 'grp', split_axis=0, concat_axis=0, tiled=T...  119 us
    all_to_all x1, blocking collectives, per_device(): lax.all_to_all(picked_keys, 'grp', split_axis=0, concat_axis=0, tiled=True)  99.4 us
    dot_general x4, matrix products, one_block(): jnp.einsum('hqk,khd->qhd', weights, values_heads, preferred_element_type=...  74.3 us
    reduce_scatter x1, waiting for transfers between devices, per_device(): lax.psum_scatter(attend(group_queries, cand_user, key_rows, values, key_u...  61.7 us
    dot_general x3, matrix products, project(): jnp.dot(normed_rows, weight, preferred_element_type=jnp.float32)  16.9 us
    dynamic_update_slice x8, local copies, waits for them, and re-layouts, attend(): lax.map(one_block, jnp.arange(row_count // block_size, dtype=jnp.int32))  14 us
    unnamed x22, local copies, waits for them, and re-layouts  13.7 us
  transfers between devices with their start and end apart: 4, of which 2 were waited for; matrix products, arithmetic and copies ran while one was open for 10% of the time, Pallas kernels for 0%

commit v1 on v0

v1 whole, which is shorter than its diff:
```python
import functools
import math

import jax
import jax.numpy as jnp
from jax import lax
from jax.experimental import pallas as pl
from jax.experimental.pallas import tpu as pltpu
from jax.sharding import PartitionSpec as P

HEADS = 8
BPS = 8
NORM_EPS = 1e-06
LAYER_EPS = 1e-05
MESH = pl.DeviceIdType.MESH
F32 = jnp.float32
BF16 = jnp.bfloat16


def rms_rows(block_rows):
    widened = block_rows.astype(F32)
    return widened * lax.rsqrt(jnp.mean(widened * widened, axis=-1, keepdims=True) + NORM_EPS)


def silu(v):
    half = 0.5 * v
    return half + half * jnp.tanh(half)


def attend_kernel(group, first, meta, raw, q_ref, usr_ref, wk_ref, wv_ref, *rest):
    if first:
        out_ref, keys, values, xbuf, total, sem = rest
    else:
        acc_ref, out_ref, keys, values, xbuf, total, sem = rest
    rows, width = q_ref.shape
    blk = raw.shape[1]
    span = group * blk
    head = width // HEADS
    tile = 512
    scale = 0.5 / math.sqrt(head)

    if first:
        total[...] = jnp.zeros_like(total)
    else:
        total[...] = acc_ref[...].astype(F32)

    def fetch(user, chunk, slot):
        return [
            pltpu.make_async_copy(
                raw.at[meta[2 + user * BPS + chunk * group + i]],
                xbuf.at[slot, pl.ds(i * blk, blk)],
                sem.at[slot, i],
            )
            for i in range(group)
        ]

    for user in range(2):
        chunks = (meta[user] + group - 1) // group

        @pl.when(chunks > 0)
        def _():
            for c in fetch(user, 0, 0):
                c.start()

        @pl.loop(0, chunks)
        def _(chunk):
            slot = lax.rem(chunk, 2)

            @pl.when(chunk + 1 < chunks)
            def _():
                for c in fetch(user, chunk + 1, 1 - slot):
                    c.start()

            for c in fetch(user, chunk, slot):
                c.wait()
            normed = rms_rows(xbuf[slot]).astype(BF16)
            base = pl.multiple_of(user * BPS * blk + chunk * span, span)
            keys[pl.ds(base, span), :] = silu(
                jnp.dot(normed, wk_ref[...], preferred_element_type=F32)
            ).astype(BF16)
            projected = silu(jnp.dot(normed, wv_ref[...], preferred_element_type=F32))
            within = lax.broadcasted_iota(jnp.int32, (blk, 1), 0)
            for i in range(group):
                ok = within < meta[2 + 2 * BPS + user * BPS + chunk * group + i]
                values[pl.ds(base + i * blk, blk), :] = jnp.where(
                    ok, projected[i * blk : (i + 1) * blk], 0.0
                ).astype(BF16)

        @pl.loop(0, rows // tile)
        def _(t):
            at = pl.ds(pl.multiple_of(t * tile, tile), tile)
            mine = usr_ref[at, :] == user

            @pl.loop(0, chunks)
            def _(chunk):
                base = pl.multiple_of(user * BPS * blk + chunk * span, span)
                for h in range(HEADS):
                    cols = slice(h * head, (h + 1) * head)
                    qh = jnp.where(mine, q_ref[at, cols], jnp.zeros((), BF16))
                    scores = lax.dot_general(
                        qh,
                        keys[pl.ds(base, span), cols],
                        (((1,), (1,)), ((), ())),
                        preferred_element_type=F32,
                    )
                    half = (scores * scale).astype(BF16)
                    weights = half + half * jnp.tanh(half)
                    total[at, cols] += jnp.dot(
                        weights, values[pl.ds(base, span), cols], preferred_element_type=F32
                    )

    out_ref[...] = total[...].astype(BF16)


def attend(meta, raw, queries, users, w_key, w_value, partial, group):
    rows, width = queries.shape
    blk = raw.shape[1]
    first = partial is None
    vmem = pl.BlockSpec(memory_space=pltpu.VMEM)
    args = (meta, raw, queries, users, w_key, w_value) + (() if first else (partial,))
    specs = [pl.BlockSpec(memory_space=pltpu.SMEM), pl.BlockSpec(memory_space=pl.ANY)]
    specs += [vmem] * (len(args) - 2)
    cost = 6e9 * 4 if first else 4e9
    return pl.pallas_call(
        functools.partial(attend_kernel, group, first),
        out_shape=jax.ShapeDtypeStruct((rows, width), BF16),
        in_specs=specs,
        out_specs=vmem,
        scratch_shapes=[
            pltpu.VMEM((2 * BPS * blk, width), BF16),
            pltpu.VMEM((2 * BPS * blk, width), BF16),
            pltpu.VMEM((2, group * blk, width), BF16),
            pltpu.VMEM((rows, width), F32),
            pltpu.SemaphoreType.DMA((2, group)),
        ],
        compiler_params=pltpu.CompilerParams(vmem_limit_bytes=56 * 2**20),
        cost_estimate=pl.CostEstimate(
            flops=int(cost), bytes_accessed=20 * 2**20, transcendentals=2**24
        ),
    )(*args)


def finish_kernel(
    part, tok_ref, normed_ref, wg_ref, wo_ref, out_ref,
    mine, give, got, folded, relay, landed, lsem, csend, crecv, zsend, zrecv,
):
    grp = lax.axis_index("grp")
    shard = lax.axis_index("hist")
    z, core = shard // 2, lax.rem(shard, 2)
    up, down, far = lax.rem(z + 1, 4), lax.rem(z + 3, 4), lax.rem(z + 2, 4)
    rows = tok_ref.shape[0]
    half = rows // 2

    def device(zz, cc):
        return (grp, zz * 2 + cc)

    barrier = pltpu.get_barrier_semaphore()
    for zz, cc in ((z, 1 - core), (up, core), (down, core)):
        pl.semaphore_signal(barrier, inc=1, device_id=device(zz, cc), device_id_type=MESH)

    order = (far, up, down, z)
    loads = []
    for i, zz in enumerate(order):
        theirs = pltpu.make_async_copy(
            part.at[pl.ds((zz * 2 + 1 - core) * rows, rows)], give.at[i], lsem.at[i]
        )
        theirs.start()
        own = pltpu.make_async_copy(
            part.at[pl.ds((zz * 2 + core) * rows, rows)], mine.at[i], lsem.at[4 + i]
        )
        own.start()
        loads.append((theirs, own))
    pl.semaphore_wait(barrier, 3)

    swaps = []
    for i in range(4):
        loads[i][0].wait()
        c = pltpu.make_async_remote_copy(
            src_ref=give.at[i],
            dst_ref=got.at[i],
            send_sem=csend.at[i],
            recv_sem=crecv.at[i],
            device_id=device(z, 1 - core),
            device_id_type=MESH,
        )
        c.start()
        swaps.append(c)

    def send(src, dst, k, zz):
        c = pltpu.make_async_remote_copy(
            src_ref=src,
            dst_ref=dst,
            send_sem=zsend.at[k],
            recv_sem=zrecv.at[k],
            device_id=device(zz, core),
            device_id_type=MESH,
        )
        c.start()
        return c

    def fold(i):
        loads[i][1].wait()
        swaps[i].wait_recv()
        folded[i] = (mine[i].astype(F32) + got[i].astype(F32)).astype(BF16)

    lo, hi = slice(0, half), slice(half, rows)
    fold(0)
    s0 = send(folded.at[0, lo], relay.at[0], 0, up)
    s1 = send(folded.at[0, hi], relay.at[1], 1, down)
    fold(1)
    s2 = send(folded.at[1, hi], landed.at[0, hi], 2, up)
    fold(2)
    s3 = send(folded.at[2, lo], landed.at[1, lo], 3, down)
    gate = silu(jnp.dot(normed_ref[...], wg_ref[...], preferred_element_type=F32))
    s0.wait_recv()
    folded[1, lo] = (folded[1, lo].astype(F32) + relay[0].astype(F32)).astype(BF16)
    s4 = send(folded.at[1, lo], landed.at[0, lo], 4, up)
    s1.wait_recv()
    folded[2, hi] = (folded[2, hi].astype(F32) + relay[1].astype(F32)).astype(BF16)
    s5 = send(folded.at[2, hi], landed.at[1, hi], 5, down)
    loads[3][1].wait()
    swaps[3].wait_recv()
    own = mine[3].astype(F32) + got[3].astype(F32)
    for s in (s2, s3, s4, s5):
        s.wait_recv()
    attn = own + landed[0].astype(F32) + landed[1].astype(F32)
    centred = attn - jnp.mean(attn, axis=-1, keepdims=True)
    normed = centred * lax.rsqrt(jnp.mean(centred * centred, axis=-1, keepdims=True) + LAYER_EPS)
    gated = (normed * gate).astype(BF16)
    mixed = tok_ref[...].astype(F32) + jnp.dot(gated, wo_ref[...], preferred_element_type=F32)
    out_ref[...] = mixed.astype(BF16)
    for s in (s0, s1, s2, s3, s4, s5):
        s.wait_send()
    for s in swaps:
        s.wait_send()


def finish(partial, tokens, normed, w_gate, w_out):
    rows, width = tokens.shape
    vmem = pl.BlockSpec(memory_space=pltpu.VMEM)
    piece = pltpu.VMEM((4, rows, width), BF16)
    return pl.pallas_call(
        finish_kernel,
        out_shape=jax.ShapeDtypeStruct((rows, width), BF16),
        in_specs=[pl.BlockSpec(memory_space=pl.ANY)] + [vmem] * 4,
        out_specs=vmem,
        scratch_shapes=[
            piece,
            piece,
            piece,
            pltpu.VMEM((3, rows, width), BF16),
            pltpu.VMEM((2, rows // 2, width), BF16),
            pltpu.VMEM((2, rows, width), BF16),
            pltpu.SemaphoreType.DMA((8,)),
            pltpu.SemaphoreType.DMA((4,)),
            pltpu.SemaphoreType.DMA((4,)),
            pltpu.SemaphoreType.DMA((6,)),
            pltpu.SemaphoreType.DMA((6,)),
        ],
        compiler_params=pltpu.CompilerParams(
            collective_id=1, has_side_effects=True, vmem_limit_bytes=48 * 2**20
        ),
        cost_estimate=pl.CostEstimate(
            flops=2 * rows * width * width * 2, bytes_accessed=12 * 2**20, transcendentals=2**18
        ),
    )(partial, tokens, normed, w_gate, w_out)


def per_device(
    cand_tokens,
    cand_user,
    hist_len,
    req_owner,
    req_slot,
    hist_embed,
    w_query,
    w_key,
    w_value,
    w_gate,
    w_out,
):
    n_grp = lax.axis_size("grp")
    shard_id = lax.axis_index("hist")
    owners = req_owner[0, 0, :, 0]
    slots = req_slot[0, 0]
    req_count = owners.shape[0]
    own_cache = hist_embed[:, 0]
    blk = own_cache.shape[1]

    order = jnp.arange(req_count, dtype=jnp.int32)
    before = (owners[None, :] == owners[:, None]) & (order[None, :] < order[:, None])
    rank = jnp.sum(before.astype(jnp.int32), axis=1)
    places = jnp.arange(n_grp * 2, dtype=jnp.int32)
    chosen = places[:, None] == (owners * 2 + rank)[None, :]
    send_slots = jnp.sum(jnp.where(chosen, slots[None, :], 0), axis=1).reshape(n_grp, 2)
    asked = lax.all_to_all(send_slots, "grp", split_axis=0, concat_axis=0, tiled=True)

    user = order // BPS
    start = (shard_id * BPS + order % BPS) * blk
    valid = jnp.clip(jnp.take(hist_len, user, axis=0) - start, 0, blk)

    def listing(wave):
        counts, idx, lens = [], [], []
        for u in range(2):
            use = (rank == wave) & (valid > 0) & (user == u)
            pos = jnp.cumsum(use.astype(jnp.int32)) - 1
            hit = use[None, :] & (pos[None, :] == jnp.arange(BPS, dtype=jnp.int32)[:, None])
            counts.append(jnp.sum(use.astype(jnp.int32))[None])
            idx.append(jnp.sum(jnp.where(hit, owners[None, :], 0), axis=1))
            lens.append(jnp.sum(jnp.where(hit, valid[None, :], 0), axis=1))
        return jnp.concatenate(counts + idx + lens)

    normed_tokens = rms_rows(cand_tokens).astype(BF16)
    queries = jax.nn.silu(jnp.dot(normed_tokens, w_query, preferred_element_type=F32)).astype(BF16)
    group_queries = lax.all_gather(queries, "hist", axis=0, tiled=True)
    users = cand_user[:, None]

    partial = None
    for wave in range(2):
        sent = jnp.take(own_cache, asked[:, wave], axis=0)
        raw = lax.all_to_all(sent, "grp", split_axis=0, concat_axis=0, tiled=True)
        partial = attend(
            listing(wave), raw, group_queries, users, w_key, w_value, partial, (4, 2)[wave]
        )
    return finish(partial, cand_tokens, normed_tokens, w_gate, w_out)


def solution(mesh):
    placed = (
        P(("grp", "hist"), None),
        P("grp"),
        P("grp"),
        P("grp", "hist", None, None),
        P("grp", "hist", None),
        P("grp", "hist", None, None),
        P(),
        P(),
        P(),
        P(),
        P(),
    )
    return jax.shard_map(
        per_device, mesh=mesh, in_specs=placed, out_specs=P(("grp", "hist"), None), check_vma=False
    )
```

time: 509 us -> 227 us (0.45)
  waiting for transfers between devices: 180 us -> 42 us
  Pallas kernels: 0 us -> 111 us
  matrix products: 96.1 us -> 1.59 us
  blocking collectives: 99.4 us -> 13.8 us
  local copies, waits for them, and re-layouts: 69.5 us -> 17 us
  other arithmetic: 32.1 us -> 17.1 us
    pallas_call x0 -> x3, Pallas kernels: none -> 111 us  [the longest x2 63 us: attend(): pl.pallas_call(functools.partial(attend_kernel, group, first), out_shape=...]
    dot_general x8 -> x1, matrix products: 96.1 us -> 1.59 us  [per_device(): jnp.dot(normed_tokens, w_query, preferred_element_type=F32)]
    all_to_all x1, blocking collectives: 99.4 us -> 13.8 us  [per_device(): lax.all_to_all(send_slots, 'grp', split_axis=0, concat_axis=0, tiled=True)]
    all_to_all x2, waiting for transfers between devices: 119 us -> 42 us  [per_device(): raw = lax.all_to_all(sent, 'grp', split_axis=0, concat_axis=0, tiled=True)]
    reduce_scatter x1 -> x0, waiting for transfers between devices: 61.7 us -> none  [per_device(): lax.psum_scatter(attend(group_queries, cand_user, key_rows, values, key_u...]
    gather x5 -> x3, local copies, waits for them, and re-layouts: 27.2 us -> 10.6 us  [the longest x2 9.95 us: per_device(): sent = jnp.take(own_cache, asked[:, wave], axis=0)]
    dynamic_update_slice x8 -> x0, local copies, waits for them, and re-layouts: 14 us -> none  [attend(): lax.map(one_block, jnp.arange(row_count // block_size, dtype=jnp.int32))]
    unnamed x22 -> x17, local copies, waits for them, and re-layouts: 13.7 us -> 0.84 us
  transfers between devices with their start and end apart: 4 -> 3, of which waited for: 2 -> 1; matrix products, arithmetic and copies ran while one was open for 10% -> 14% of each run, Pallas kernels for 0% -> 21%
where the time goes in v1:
time: 227 us; the launch traced here: 225 us
  Pallas kernels  111 us (49%)
  waiting for transfers between devices  42 us (19%)
  other arithmetic  17.1 us (8%)
  local copies, waits for them, and re-layouts  17 us (7%)
  blocking collectives  13.8 us (6%)
  between operations  13.6 us (6%)
  starting transfers between devices  9.66 us (4%)
    pallas_call x2, Pallas kernels, attend(): pl.pallas_call(functools.partial(attend_kernel, group, first), out_shape=...  63 us
    pallas_call x1, Pallas kernels, finish(): pl.pallas_call(finish_kernel, out_shape=jax.ShapeDtypeStruct((rows, width...  47.5 us
    all_to_all x2, waiting for transfers between devices, per_device(): raw = lax.all_to_all(sent, 'grp', split_axis=0, concat_axis=0, tiled=True)  42 us
    all_to_all x1, blocking collectives, per_device(): lax.all_to_all(send_slots, 'grp', split_axis=0, concat_axis=0, tiled=True)  13.8 us
    gather x2, local copies, waits for them, and re-layouts, per_device(): sent = jnp.take(own_cache, asked[:, wave], axis=0)  9.95 us
    all_to_all x2, starting transfers between devices, per_device(): raw = lax.all_to_all(sent, 'grp', split_axis=0, concat_axis=0, tiled=True)  9.66 us
    select_n x2, other arithmetic, per_device(): sent = jnp.take(own_cache, asked[:, wave], axis=0)  9.27 us
  transfers between devices with their start and end apart: 3, of which 1 were waited for; matrix products, arithmetic and copies ran while one was open for 14% of the time, Pallas kernels for 21%

profile of v1, /device:TPU:1, one launch (start us, length us, event | category | flops | bytes accessed | tf_op | source)
XLA Modules:
  0.0 225.2 jit_solution(1041247845110859647)
XLA Ops:
  6.5 1.4 fusion
  7.9 1.2 fusion.1.normed_ref
  9.2 1.6 multiply_convert_fusion
  10.8 0.6 fusion.32
  11.5 1.4 select_reduce_fusion
  12.9 0.2 convert_reduce_fusion
  13.1 0.7 convert_reduce_fusion.1
  13.7 0.1 select_reduce_fusion.1
  13.9 13.8 %all_to_all.22 = s32[16,1,2]{2,1,0:T(1,128)S(1)} all-to-all(s32[16,1,2]{2,1,0:T(1,128)S(1)} %bitcast.27), channel_id=1, replica_groups=mesh['grp'=16,'hist'=8] {'grp'}, dimensions={0} | all-to-all | bytes 256 | tf_op jit(solution)/shard_map/all_to_all | solution.py:296
  27.8 5.0 %gather_fusion.1 = bf16[16,128,1024]{2,1,0:T(8,128)(2,1)} fusion(bf16[16,128,1024]{2,1,0:T(8,128)(2,1)} %bitcast.25, s32[1024]{0:T(1024)S(1)} %pad_clamp_fusion), kind=kCustom, calls=%fused_computation.1.clone | custom fusion | bytes 8388672 | tf_op jit(solution)/shard_map/jit(_take)/gather | solution.py:320
  32.8 4.7 %broadcast_select_fusion = bf16[16,128,1024]{2,1,0:T(8,128)(2,1)} fusion(bf16[16,128,1024]{2,1,0:T(8,128)(2,1)} %gather_fusion.1, pred[16]{0:T(512)(128)(4,1)S(1)} %get-tuple-element.26), kind=kLoop, calls=%fused_computation.2 | loop fusion | flops 2097152 | bytes 8388624 | tf_op jit(solution)/shard_map/jit(_take)/select_n | solution.py:320
  37.5 4.5 %all-to-all-start.2 = ((bf16[16,128,1024]{2,1,0:T(8,128)(2,1)}), bf16[16,128,1024]{2,1,0:T(8,128)(2,1)}, u32[]{:S(2)}, u32[]{:S(2)}) async-start(bf16[16,128,1024]{2,1,0:T(8,128)(2,1)} %broadcast_select_fusion), calls=%async_computation.2 | async-start | bytes 8388608 | tf_op jit(solution)/shard_map/all_to_all | solution.py:321
  42.0 5.0 %gather_fusion = bf16[16,128,1024]{2,1,0:T(8,128)(2,1)} fusion(bf16[16,128,1024]{2,1,0:T(8,128)(2,1)} %bitcast.26, s32[1024]{0:T(1024)S(1)} %pad_clamp_fusion.1), kind=kCustom, calls=%fused_computation.clone | custom fusion | bytes 8388672 | tf_op jit(solution)/shard_map/jit(_take)/gather | solution.py:320
  47.0 4.6 %broadcast_select_fusion.1 = bf16[16,128,1024]{2,1,0:T(8,128)(2,1)} fusion(bf16[16,128,1024]{2,1,0:T(8,128)(2,1)} %gather_fusion, pred[16]{0:T(512)(128)(4,1)S(1)} %get-tuple-element.43), kind=kLoop, calls=%fused_computation.3 | loop fusion | flops 2097152 | bytes 8388624 | tf_op jit(solution)/shard_map/jit(_take)/select_n | solution.py:320
  51.6 42.0 %all-to-all-done.2.raw = bf16[16,128,1024]{2,1,0:T(8,128)(2,1)} async-done(((bf16[16,128,1024]{2,1,0:T(8,128)(2,1)}), bf16[16,128,1024]{2,1,0:T(8,128)(2,1)}, u32[]{:S(2)}, u32[]{:S(2)}) %all-to-all-start.2) | async-done | bytes 4194336 | tf_op jit(solution)/shard_map/all_to_all | solution.py:321
  93.6 5.1 %all-to-all-start.1 = ((bf16[16,128,1024]{2,1,0:T(8,128)(2,1)}), bf16[16,128,1024]{2,1,0:T(8,128)(2,1)}, u32[]{:S(2)}, u32[]{:S(2)}) async-start(bf16[16,128,1024]{2,1,0:T(8,128)(2,1)} %broadcast_select_fusion.1), calls=%async_computation.1 | async-start | bytes 8388608 | tf_op jit(solution)/shard_map/all_to_all | solution.py:321
  98.7 0.1 copy.26
  98.8 0.1 copy.29
  98.9 1.3 and_convert_fusion
  100.4 1.4 copy.31.usr_ref
  101.7 0.1 add_reduce_fusion
  101.8 0.1 add_reduce_fusion.1
  102.0 0.1 add_reduce_fusion.2
  102.1 0.1 add_reduce_fusion.3
  102.2 0.7 convert_reduce_fusion.2
  102.9 0.2 select_reduce_fusion.7
  103.2 1.9 concatenate.7.meta
  105.0 2.0 concatenate.6.meta
  107.0 46.3 %shard_map.109.rest_0_ = bf16[2048,1024]{1,0:T(8,128)(2,1)} custom-call(s32[34]{0:T(128)} %concatenate.7.meta, bf16[16,128,1024]{2,1,0:T(8,128)(2,1)} %all-to-all-done.2.raw, bf16[2048,1024]{1,0:T(8,128)(2,1)} %all-gather.2.cloned.1.call-done.q_ref, s32[2048,1]{1,0:T(8,128)} %copy.31.usr_ref, bf16[1024,1024]{1,0:T(8,128)(2,1)} %wk_ref.3, ...), custom_call_target="tpu_custom_call" | custom-call | flops 24000000000 | bytes 20971520 | tf_op jit(solution)/shard_map/pallas_call | solution.py:124
  153.4 16.7 %shard_map.110.part = bf16[2048,1024]{1,0:T(8,128)(2,1)} custom-call(s32[34]{0:T(128)} %concatenate.6.meta, bf16[16,128,1024]{2,1,0:T(8,128)(2,1)} %all-to-all-done.1.raw, bf16[2048,1024]{1,0:T(8,128)(2,1)} %all-gather.2.cloned.1.call-done.q_ref, s32[2048,1]{1,0:T(8,128)} %copy.31.usr_ref, bf16[1024,1024]{1,0:T(8,128)(2,1)} %wk_ref.3, ...), custom_call_target="tpu_custom_call" | custom-call | flops 4000000000 | bytes 20971520 | tf_op jit(solution)/shard_map/pallas_call | solution.py:124
  170.1 47.5 %shard_map.111 = bf16[256,1024]{1,0:T(8,128)(2,1)S(1)} custom-call(bf16[2048,1024]{1,0:T(8,128)(2,1)} %shard_map.110.part, bf16[256,1024]{1,0:T(8,128)(2,1)S(1)} %copy-done.1, bf16[256,1024]{1,0:T(8,128)(2,1)S(1)} %fusion.1.normed_ref, bf16[1024,1024]{1,0:T(8,128)(2,1)S(1)} %copy-done.2, bf16[1024,1024]{1,0:T(8,128)(2,1)S(1)} %copy-done.3), custom_call_target="tpu_custom_call" | custom-call | flops 1073741824 | bytes 12582912 | tf_op jit(solution)/shard_map/pallas_call | solution.py:242
  217.6 0.8 copy.33
  (31 shorter events, 0.4 us)
Async XLA Ops:
  6.5 2.6 %copy-start = (bf16[1024,1024]{1,0:T(8,128)(2,1)S(1)}, bf16[1024,1024]{1,0:T(8,128)(2,1)}, u32[]{:S(2)}) copy-start(bf16[1024,1024]{1,0:T(8,128)(2,1)} %param.19) | copy-start | bytes 6291460
  6.5 100.4 %all-gather.2.cloned.1.call-start = ((), (), s32[]{:S(2)}) async-start(), calls=%async_computation.3 | async-start | bytes 4718592 | tf_op jit(solution)/shard_map/all_gather | solution.py:315
  9.1 1.7 copy-start.5
  9.1 3.7 %copy-start.6 = (s32[1,1,16,1]{2,3,1,0:T(1,128)S(1)}, s32[1,1,16,1]{2,3,1,0:T(1,128)}, u32[]{:S(2)}) copy-start(s32[1,1,16,1]{2,3,1,0:T(1,128)} %param.16) | copy-start | bytes 196
  9.2 4.6 %copy-start.7 = (s32[1,1,16]{2,1,0:T(1,128)S(1)}, s32[1,1,16]{2,1,0:T(1,128)}, u32[]{:S(2)}) copy-start(s32[1,1,16]{2,1,0:T(1,128)} %param.17) | copy-start | bytes 196
  37.5 56.1 %all-to-all-start.2 = ((bf16[16,128,1024]{2,1,0:T(8,128)(2,1)}), bf16[16,128,1024]{2,1,0:T(8,128)(2,1)}, u32[]{:S(2)}, u32[]{:S(2)}) async-start(bf16[16,128,1024]{2,1,0:T(8,128)(2,1)} %broadcast_select_fusion), calls=%async_computation.2 | async-start | bytes 8388608 | tf_op jit(solution)/shard_map/all_to_all | solution.py:321
  51.6 48.8 %copy-start.4 = (s32[2048]{0:T(1024)S(1)}, s32[2048]{0:T(1024)}, u32[]{:S(2)}) copy-start(s32[2048]{0:T(1024)} %param.14) | copy-start | bytes 24580
  93.6 59.7 %all-to-all-start.1 = ((bf16[16,128,1024]{2,1,0:T(8,128)(2,1)}), bf16[16,128,1024]{2,1,0:T(8,128)(2,1)}, u32[]{:S(2)}, u32[]{:S(2)}) async-start(bf16[16,128,1024]{2,1,0:T(8,128)(2,1)} %broadcast_select_fusion.1), calls=%async_computation.1 | async-start | bytes 8388608 | tf_op jit(solution)/shard_map/all_to_all | solution.py:321
  153.3 16.7 %copy-start.1 = (bf16[256,1024]{1,0:T(8,128)(2,1)S(1)}, bf16[256,1024]{1,0:T(8,128)(2,1)}, u32[]{:S(2)}) copy-start(bf16[256,1024]{1,0:T(8,128)(2,1)} %tok_ref.1) | copy-start | bytes 1572868
  153.3 16.7 %copy-start.2 = (bf16[1024,1024]{1,0:T(8,128)(2,1)S(1)}, bf16[1024,1024]{1,0:T(8,128)(2,1)}, u32[]{:S(2)}) copy-start(bf16[1024,1024]{1,0:T(8,128)(2,1)} %wg_ref.1) | copy-start | bytes 6291460
  153.4 16.7 %copy-start.3 = (bf16[1024,1024]{1,0:T(8,128)(2,1)S(1)}, bf16[1024,1024]{1,0:T(8,128)(2,1)}, u32[]{:S(2)}) copy-start(bf16[1024,1024]{1,0:T(8,128)(2,1)} %wo_ref.1) | copy-start | bytes 6291460
Sparse Core Ops, SparseCore 0:
  10.9 35.9 all-gather.1

commit v2 on v0

v2 whole, which is shorter than its diff:
```python
import math

import jax
import jax.numpy as jnp
from jax import lax
from jax.experimental import pallas as pl
from jax.experimental.pallas import tpu as pltpu
from jax.sharding import PartitionSpec as P

HEADS = 8
BPS = 8
SIDE = 4
NORM_EPS = 1e-06
LAYER_EPS = 1e-05
MESH = pl.DeviceIdType.MESH
F32 = jnp.float32
BF16 = jnp.bfloat16

NEAR = ((1, 0), (3, 0), (0, 1), (0, 3))
DIAG = ((1, 1), (3, 3), (1, 3), (3, 1))
LONG = ((2, 1), (1, 2), (2, 3), (3, 2))
OPPOSITE = ((2, 2),)
STRAIGHT = ((2, 0), (0, 2))
OFFSETS = ((0, 0),) + NEAR + DIAG + LONG + OPPOSITE + STRAIGHT
SETS = (((1, 9), (9, 16)), ((1, 9), (9, 13), (13, 14), (14, 16)))
PIECES = 4
PRE = 4


def rms_rows(block_rows):
    widened = block_rows.astype(F32)
    return widened * lax.rsqrt(jnp.mean(widened * widened, axis=-1, keepdims=True) + NORM_EPS)


def silu(v):
    half = 0.5 * v
    return half + half * jnp.tanh(half)


def layer_kernel(
    tab, late, tok_ref, usr_ref, cache_hbm, wq_hbm, wk_hbm, wv_hbm, wg_hbm, wo_hbm, out_ref,
    cache, wq, wk, wv, ask_out, ask_in, asked, stage, recv, landed, q_all, umask, keys, vals, total,
    mine, give, got, folded, relay, final,
    wsem, asend, arecv, ssem, rsem, qsend, qrecv, csend, crecv, zsend, zrecv,
):
    grp = lax.axis_index("grp")
    shard = lax.axis_index("hist")
    gx, gy = grp // SIDE, lax.rem(grp, SIDE)
    z, core = shard // 2, lax.rem(shard, 2)
    up, down, far = lax.rem(z + 1, SIDE), lax.rem(z + 3, SIDE), lax.rem(z + 2, SIDE)
    rows, width = tok_ref.shape
    blk = cache.shape[1]
    head = width // HEADS
    slots = len(OFFSETS)
    half = rows // 2

    def across(dx, dy):
        return (lax.rem(gx + dx, SIDE) * SIDE + lax.rem(gy + dy, SIDE), shard)

    def back(p):
        return across((SIDE - OFFSETS[p][0]) % SIDE, (SIDE - OFFSETS[p][1]) % SIDE)

    def along(zz, cc):
        return (grp, zz * 2 + cc)

    def remote(src, dst, send_sem, recv_sem, device):
        return pltpu.make_async_remote_copy(
            src_ref=src, dst_ref=dst, send_sem=send_sem, recv_sem=recv_sem, device_id=device, device_id_type=MESH
        )

    loads = []
    for i, (src, dst) in enumerate(
        ((cache_hbm, cache), (wq_hbm, wq), (wk_hbm, wk), (wv_hbm, wv))
    ):
        c = pltpu.make_async_copy(src, dst, wsem.at[i])
        c.start()
        loads.append(c)

    barrier = pltpu.get_barrier_semaphore()
    partners = [across(*o) for o in OFFSETS[1:]] + [along(z, 1 - core), along(up, core), along(down, core)]
    for device in partners:
        pl.semaphore_signal(barrier, inc=1, device_id=device, device_id_type=MESH)
    pl.semaphore_wait(barrier, len(partners))

    lane = lax.broadcasted_iota(jnp.int32, (1, 128), 1)
    for p in range(slots):
        ask_out[p] = jnp.where(lane == 0, tab[p, 0], jnp.where(lane == 1, tab[p, 3], 0))
    asks = []
    for p in range(1, slots):
        c = remote(ask_out.at[p], ask_in.at[p], asend.at[p], arecv.at[p], back(p))
        c.start()
        asks.append(c)
    ask_in[0] = ask_out[0]

    def q_rows(zz, cc, first=0, count=None):
        return q_all.at[pl.ds(pl.multiple_of((zz * 2 + cc) * rows + first, half), count or rows)]

    def hop(k, src, device):
        c = remote(src, src, qsend.at[k], qrecv.at[k], device)
        c.start()
        return c

    normed_tokens = rms_rows(tok_ref[...]).astype(BF16)
    loads[1].wait()
    q_all[pl.ds(pl.multiple_of(shard * rows, rows), rows), :] = silu(
        jnp.dot(normed_tokens, wq[...], preferred_element_type=F32)
    ).astype(BF16)
    to_up = hop(0, q_rows(z, core), along(up, core))
    to_down = hop(1, q_rows(z, core), along(down, core))
    to_side = hop(2, q_rows(z, core), along(z, 1 - core))

    for c in asks:
        c.wait_recv()
    c = pltpu.make_async_copy(ask_in, asked, wsem.at[6])
    c.start()
    c.wait()
    loads[0].wait()
    recv[0] = cache[asked[0, 0, 0]]
    landed[0] = cache[asked[0, 0, 1]]
    step = blk // PIECES
    for wave in range(2):
        for first, last in SETS[wave]:
            for p in range(first, last):
                stage[wave * slots + p] = cache[asked[p, 0, wave]]
            for piece in range(PIECES):
                part = pl.ds(piece * step, step)
                for p in range(first, last):
                    s = wave * slots + p
                    remote(
                        stage.at[s, part], recv.at[s, part], ssem.at[s], rsem.at[s], across(*OFFSETS[p])
                    ).start()

    blocks = width // blk
    for i, src in enumerate((wg_hbm, wo_hbm)):
        c = pltpu.make_async_copy(src, cache.at[pl.ds(i * blocks, blocks)], wsem.at[4 + i])
        c.start()
        loads.append(c)

    def late_weight(i):
        loads[4 + i].wait()
        return cache[pl.ds(i * blocks, blocks)].reshape(width, width)

    def whole(s):
        return remote(stage.at[s], recv.at[s], ssem.at[s], rsem.at[s], along(z, 1 - core))

    for i in range(usr_ref.shape[0]):
        line = jnp.broadcast_to(usr_ref[i : i + 1, :].astype(F32), (128, 128))
        umask[pl.ds(i * 128, 128), :] = line.T

    to_up.wait_recv()
    on_up = hop(3, q_rows(down, core, 0, half), along(up, core))
    side_down = hop(4, q_rows(down, core), along(z, 1 - core))
    to_down.wait_recv()
    on_down = hop(5, q_rows(up, core, half, half), along(down, core))
    side_up = hop(6, q_rows(up, core), along(z, 1 - core))

    def project(x, k, n0, n1):
        normed = rms_rows(x).astype(BF16)
        keys[k] = silu(jnp.dot(normed, wk[...], preferred_element_type=F32)).astype(BF16)
        projected = silu(jnp.dot(normed, wv[...], preferred_element_type=F32)).astype(BF16)
        within = lax.broadcasted_iota(jnp.int32, (blk, 1), 0)
        zero = jnp.zeros((), BF16)
        for i in range(2):
            here = slice(i * blk, (i + 1) * blk)
            left = jnp.where(within < n0[i], projected[here], zero)
            right = jnp.where(within < n1[i], projected[here], zero)
            for h in range(HEADS):
                cols = slice(h * head, (h + 1) * head)
                vals[k, here, 2 * h * head : (2 * h + 1) * head] = left[:, cols]
                vals[k, here, (2 * h + 1) * head : (2 * h + 2) * head] = right[:, cols]

    tile = 2 * rows
    scale = 0.5 / math.sqrt(head)

    def attend_tile(zz, k, fresh=False):
        at = pl.ds(pl.multiple_of(zz * tile, tile), tile)
        first_user = umask[at, :] == 0.0
        for h in range(HEADS):
            cols = slice(h * head, (h + 1) * head)
            scores = lax.dot_general(
                q_all[at, cols], keys[k, :, cols], (((1,), (1,)), ((), ())), preferred_element_type=F32
            )
            part = (scores * scale).astype(BF16)
            weights = part + part * jnp.tanh(part)
            both = jnp.dot(
                weights, vals[k, :, 2 * h * head : (2 * h + 2) * head], preferred_element_type=F32
            )
            total[at, cols] += jnp.where(first_user, both[:, :head], both[:, head:])

    def pair(buffer, base):
        return buffer[pl.ds(base, 2)].reshape(2 * blk, width)

    def arrive(s):
        whole(s).wait_recv()

    def wave0_keys(k, buffer):
        arrive(2 * k + 1)
        project(
            pair(recv, 2 * k), buffer,
            (tab[2 * k, 1], tab[2 * k + 1, 1]), (tab[2 * k, 2], tab[2 * k + 1, 2]),
        )

    loads[2].wait()
    loads[3].wait()
    wave0_keys(0, 0)

    @pl.loop(1, PRE)
    def _(k):
        arrive(2 * k)
        wave0_keys(k, k)

    total[...] = jnp.zeros_like(total)
    on_up.wait_recv()
    on_down.wait_recv()
    side_far = hop(7, q_rows(far, core), along(z, 1 - core))
    for c in (to_side, side_down, side_up, side_far):
        c.wait_recv()

    @pl.loop(0, PRE)
    def _(k):
        @pl.loop(0, SIDE)
        def _(zz):
            attend_tile(zz, k)

    @pl.loop(PRE, slots // 2)
    def _(k):
        arrive(2 * k)
        wave0_keys(k, 0)

        @pl.loop(0, SIDE)
        def _(zz):
            attend_tile(zz, 0)

    def land(p):
        arrive(slots + p)
        landed[p] = recv[slots + p]

    def wave1_keys(k):
        a, b = 2 * k, 2 * k + 1
        x = jnp.concatenate([landed[late[a, 0]], landed[late[b, 0]]], axis=0)
        project(x, 0, (late[a, 1], late[b, 1]), (late[a, 2], late[b, 2]))

    @pl.loop(1, slots // 2)
    def _(p):
        land(p)

    @pl.loop(0, slots // 4 - 1)
    def _(k):
        land(slots // 2 + 2 * k)
        land(slots // 2 + 2 * k + 1)
        wave1_keys(k)

        @pl.loop(0, SIDE)
        def _(zz):
            attend_tile(zz, 0)

    land(slots - 2)
    land(slots - 1)
    wave1_keys(slots // 4 - 1)

    swaps = []
    for i, zz in enumerate((far, up, down, z)):
        attend_tile(zz, 0)
        for cc, dst in ((1 - core, give), (core, mine)):
            at = pl.ds(pl.multiple_of((zz * 2 + cc) * rows, rows), rows)
            sums = total[at, :]
            dst[i] = (sums - jnp.mean(sums, axis=-1, keepdims=True)).astype(BF16)
        c = remote(give.at[i], got.at[i], csend.at[i], crecv.at[i], along(z, 1 - core))
        c.start()
        swaps.append(c)

    def send(k, src, dst, zz):
        c = remote(src, dst, zsend.at[k], zrecv.at[k], along(zz, core))
        c.start()
        return c

    def fold(i):
        swaps[i].wait_recv()
        folded[i] = (mine[i].astype(F32) + got[i].astype(F32)).astype(BF16)

    lo, hi = pl.ds(0, half), pl.ds(half, half)
    fold(0)
    s0 = send(0, folded.at[0, lo], relay.at[0], up)
    s1 = send(1, folded.at[0, hi], relay.at[1], down)
    fold(1)
    s2 = send(2, folded.at[1, hi], final.at[0, hi], up)
    fold(2)
    s3 = send(3, folded.at[2, lo], final.at[1, lo], down)
    gate = silu(jnp.dot(normed_tokens, late_weight(0), preferred_element_type=F32))
    s0.wait_recv()
    folded[1, lo] = (folded[1, lo].astype(F32) + relay[0].astype(F32)).astype(BF16)
    s4 = send(4, folded.at[1, lo], final.at[0, lo], up)
    s1.wait_recv()
    folded[2, hi] = (folded[2, hi].astype(F32) + relay[1].astype(F32)).astype(BF16)
    s5 = send(5, folded.at[2, hi], final.at[1, hi], down)
    swaps[3].wait_recv()
    own = mine[3].astype(F32) + got[3].astype(F32)
    for s in (s2, s3, s4, s5):
        s.wait_recv()
    attn = own + final[0].astype(F32) + final[1].astype(F32)
    centred = attn - jnp.mean(attn, axis=-1, keepdims=True)
    normed = centred * lax.rsqrt(jnp.mean(centred * centred, axis=-1, keepdims=True) + LAYER_EPS)
    gated = (normed * gate).astype(BF16)
    mixed = tok_ref[...].astype(F32) + jnp.dot(gated, late_weight(1), preferred_element_type=F32)
    out_ref[...] = mixed.astype(BF16)

    for c in asks + [to_up, to_down, to_side, on_up, side_down, on_down, side_up, side_far] + swaps:
        c.wait_send()
    for c in (s0, s1, s2, s3, s4, s5):
        c.wait_send()
    for wave in range(2):

        @pl.loop(1, slots)
        def _(p):
            whole(wave * slots + p).wait_send()


def per_device(
    cand_tokens,
    cand_user,
    hist_len,
    req_owner,
    req_slot,
    hist_embed,
    w_query,
    w_key,
    w_value,
    w_gate,
    w_out,
):
    rows, width = cand_tokens.shape
    grp = lax.axis_index("grp")
    shard_id = lax.axis_index("hist")
    owners = req_owner[0, 0, :, 0]
    slots = req_slot[0, 0]
    req_count = owners.shape[0]
    own_cache = hist_embed[:, 0]
    blk = own_cache.shape[1]
    positions = len(OFFSETS)

    order = jnp.arange(req_count, dtype=jnp.int32)
    before = (owners[None, :] == owners[:, None]) & (order[None, :] < order[:, None])
    rank = jnp.sum(before.astype(jnp.int32), axis=1)
    user = order // BPS
    start = (shard_id * BPS + order % BPS) * blk
    valid = jnp.clip(jnp.where(user == 0, hist_len[0], hist_len[1]) - start, 0, blk)
    facts = jnp.stack([slots, jnp.where(user == 0, valid, 0), jnp.where(user == 1, valid, 0)])
    dx = jnp.array([o[0] for o in OFFSETS], jnp.int32)
    dy = jnp.array([o[1] for o in OFFSETS], jnp.int32)
    owner_at = (grp // SIDE - dx + SIDE) % SIDE * SIDE + (grp % SIDE - dy + SIDE) % SIDE
    chosen = (owners[None, None, :] == owner_at[:, None, None]) & (
        rank[None, None, :] == jnp.arange(2, dtype=jnp.int32)[None, :, None]
    )
    tab = jnp.sum(jnp.where(chosen[:, :, None, :], facts[None, None], 0), axis=-1)
    real = tab[:, 1, 1] + tab[:, 1, 2] > 0
    place = jnp.arange(positions, dtype=jnp.int32)
    behind = jnp.sum((real[None, :] & (place[None, :] > place[:, None])).astype(jnp.int32), axis=1)
    entry = jnp.arange(positions // 2, dtype=jnp.int32)
    hit = real[None, :] & (positions // 2 - 1 - behind[None, :] == entry[:, None])
    found = jnp.stack([place, tab[:, 1, 1], tab[:, 1, 2]])
    late = jnp.sum(jnp.where(hit[:, None, :], found[None], 0), axis=-1)

    smem = pl.BlockSpec(memory_space=pltpu.SMEM)
    vmem = pl.BlockSpec(memory_space=pltpu.VMEM)
    hbm = pl.BlockSpec(memory_space=pl.ANY)
    group = cand_user.shape[0]
    weight = pltpu.VMEM((width, width), BF16)
    piece = pltpu.VMEM((SIDE, rows, width), BF16)
    dma = pltpu.SemaphoreType.DMA
    return pl.pallas_call(
        layer_kernel,
        out_shape=jax.ShapeDtypeStruct((rows, width), BF16),
        in_specs=[smem, smem, vmem, vmem] + [hbm] * 6,
        out_specs=vmem,
        scratch_shapes=[
            pltpu.VMEM(own_cache.shape, BF16),
            weight, weight, weight,
            pltpu.VMEM((positions, 1, 128), jnp.int32),
            pltpu.VMEM((positions, 1, 128), jnp.int32),
            pltpu.SMEM((positions, 1, 128), jnp.int32),
            pltpu.VMEM((2 * positions, blk, width), BF16),
            pltpu.VMEM((2 * positions, blk, width), BF16),
            pltpu.VMEM((positions, blk, width), BF16),
            pltpu.VMEM((group, width), BF16),
            pltpu.VMEM((group, 128), F32),
            pltpu.VMEM((PRE, 2 * blk, width), BF16),
            pltpu.VMEM((PRE, 2 * blk, 2 * width), BF16),
            pltpu.VMEM((group, width), F32),
            piece, piece, piece,
            pltpu.VMEM((3, rows, width), BF16),
            pltpu.VMEM((2, rows // 2, width), BF16),
            pltpu.VMEM((2, rows, width), BF16),
            dma((7,)),
            dma((positions,)), dma((positions,)),
            dma((2 * positions,)), dma((2 * positions,)),
            dma((8,)), dma((8,)),
            dma((4,)), dma((4,)),
            dma((6,)), dma((6,)),
        ],
        compiler_params=pltpu.CompilerParams(
            collective_id=1, has_side_effects=True, vmem_limit_bytes=63 * 2**20
        ),
        cost_estimate=pl.CostEstimate(
            flops=int(4e10), bytes_accessed=32 * 2**20, transcendentals=2**24
        ),
    )(
        tab.reshape(positions, 6), late, cand_tokens, cand_user.reshape(group // 128, 128), own_cache,
        w_query, w_key, w_value, w_gate.reshape(-1, blk, width), w_out.reshape(-1, blk, width),
    )


def solution(mesh):
    placed = (
        P(("grp", "hist"), None),
        P("grp"),
        P("grp"),
        P("grp", "hist", None, None),
        P("grp", "hist", None),
        P("grp", "hist", None, None),
        P(),
        P(),
        P(),
        P(),
        P(),
    )
    return jax.shard_map(
        per_device, mesh=mesh, in_specs=placed, out_specs=P(("grp", "hist"), None), check_vma=False
    )
```

time: 509 us -> 182 us (0.36)
  waiting for transfers between devices: 180 us -> 0 us
  Pallas kernels: 0 us -> 172 us
  blocking collectives: 99.4 us -> 0 us
  matrix products: 96.1 us -> 0 us
  local copies, waits for them, and re-layouts: 69.5 us -> 4.64 us
  other arithmetic: 32.1 us -> 4.83 us
  starting transfers between devices: 14.2 us -> 0 us
  between operations: 13.6 us -> 0.06 us
    pallas_call x0 -> x1, Pallas kernels: none -> 172 us  [per_device(): pl.pallas_call(layer_kernel, out_shape=jax.ShapeDtypeStruct((rows, width)...]
    all_to_all x2 -> x0, waiting for transfers between devices: 119 us -> none  [the longest x1 119 us: per_device(): lax.all_to_all(picked_values, 'grp', split_axis=0, concat_axis=0, tiled=T...]
    all_to_all x1 -> x0, blocking collectives: 99.4 us -> none  [per_device(): lax.all_to_all(picked_keys, 'grp', split_axis=0, concat_axis=0, tiled=True)]
    dot_general x8 -> x0, matrix products: 96.1 us -> none  [the longest x4 74.3 us: one_block(): jnp.einsum('hqk,khd->qhd', weights, values_heads, preferred_element_type=...]
    reduce_scatter x1 -> x0, waiting for transfers between devices: 61.7 us -> none  [per_device(): lax.psum_scatter(attend(group_queries, cand_user, key_rows, values, key_u...]
    gather x5 -> x0, local copies, waits for them, and re-layouts: 27.2 us -> none  [the longest x1 7.18 us: per_device(): jnp.take(keys_owned, asked_slots, axis=0)]
    dynamic_update_slice x8 -> x0, local copies, waits for them, and re-layouts: 14 us -> none  [attend(): lax.map(one_block, jnp.arange(row_count // block_size, dtype=jnp.int32))]
    all_to_all x2 -> x0, starting transfers between devices: 13.9 us -> none  [the longest x1 7.58 us: per_device(): lax.all_to_all(send_slots, 'grp', split_axis=0, concat_axis=0, tiled=True)]
  transfers between devices with their start and end apart: 4 -> 0, of which waited for: 2 -> 0; matrix products, arithmetic and copies ran while one was open for 10% -> 0% of each run, Pallas kernels for 0% -> 0%
where the time goes in v2:
time: 182 us; the launch traced here: 181 us
  Pallas kernels  172 us (95%)
  other arithmetic  4.83 us (3%)
  local copies, waits for them, and re-layouts  4.64 us (3%)
    pallas_call x1, Pallas kernels, per_device(): pl.pallas_call(layer_kernel, out_shape=jax.ShapeDtypeStruct((rows, width)...  172 us

profile of v2, /device:TPU:1, one launch (start us, length us, event | category | flops | bytes accessed | tf_op | source)
XLA Modules:
  0.0 181.3 jit_solution(8009343162339607274)
XLA Ops:
  0.0 0.7 fusion.3
  0.7 0.9 convert_reduce_fusion.1
  1.6 1.4 fusion.11
  3.0 1.3 compare_select_fusion.4
  4.4 0.7 pad_add_fusion
  5.0 0.7 broadcast_compare_fusion
  5.8 0.2 select_reduce_fusion
  6.0 0.1 convert_reduce_fusion
  6.2 0.1 select_reduce_fusion.1
  6.3 0.7 copy.17.late
  7.0 0.7 copy.16.tab
  7.7 171.8 %shard_map.127 = bf16[256,1024]{1,0:T(8,128)(2,1)} custom-call(s32[16,6]{1,0:T(8,128)} %copy.16.tab, s32[8,3]{1,0:T(8,128)} %copy.17.late, bf16[256,1024]{1,0:T(8,128)(2,1)} %tok_ref.1, s32[16,128]{1,0:T(8,128)} %bitcast.22, bf16[16,128,1024]{2,1,0:T(8,128)(2,1)} %bitcast.19, bf16[1024,1024]{1,0:T(8,128)(2,1)} %wq_hbm.1, bf16[1024,1024]{1,0:T(8,128)(2,1)} %wk_hbm.1, ...), custom_call_target="tpu_custom_call" | custom-call | flops 40000000000 | bytes 33554432 | tf_op jit(solution)/shard_map/pallas_call | solution.py:370
  179.4 1.9 %copy.19 = bf16[256,1024]{1,0:T(8,128)(2,1)} copy(bf16[256,1024]{1,0:T(8,128)(2,1)} %shard_map.127) | data formatting | bytes 1048576
  (9 shorter events, 0.1 us)

commit v3 on v2

--- a/solution.py
+++ b/solution.py
@@ -16,15 +16,19 @@
 F32 = jnp.float32
 BF16 = jnp.bfloat16
 
-NEAR = ((1, 0), (3, 0), (0, 1), (0, 3))
-DIAG = ((1, 1), (3, 3), (1, 3), (3, 1))
-LONG = ((2, 1), (1, 2), (2, 3), (3, 2))
-OPPOSITE = ((2, 2),)
-STRAIGHT = ((2, 0), (0, 2))
-OFFSETS = ((0, 0),) + NEAR + DIAG + LONG + OPPOSITE + STRAIGHT
-SETS = (((1, 9), (9, 16)), ((1, 9), (9, 13), (13, 14), (14, 16)))
+OFFSETS = (
+    ((0, 0),)
+    + ((1, 0), (3, 0), (0, 1), (0, 3))
+    + ((1, 1), (3, 3), (1, 3), (3, 1))
+    + ((2, 1), (2, 3), (0, 2))
+    + ((1, 2), (3, 2), (2, 0))
+    + ((2, 2),)
+)
+SETS = ((1, 9), (9, 12), (12, 15), (15, 16))
 PIECES = 4
 PRE = 4
+DUE = (0, 2, 4, 5)
+TILE = 2048
 
 
 def rms_rows(block_rows):
@@ -38,9 +42,9 @@
 
 
 def layer_kernel(
-    tab, late, tok_ref, usr_ref, cache_hbm, wq_hbm, wk_hbm, wv_hbm, wg_hbm, wo_hbm, out_ref,
+    owners, wanted, lengths, tok_ref, usr_ref, cache_hbm, wq_hbm, wk_hbm, wv_hbm, wg_hbm, wo_hbm, out_ref,
     cache, wq, wk, wv, ask_out, ask_in, asked, stage, recv, landed, q_all, umask, keys, vals, total,
-    mine, give, got, folded, relay, final,
+    mine, give, got, folded, relay, final, tab, late,
     wsem, asend, arecv, ssem, rsem, qsend, qrecv, csend, crecv, zsend, zrecv,
 ):
     grp = lax.axis_index("grp")
@@ -70,7 +74,7 @@
 
     loads = []
     for i, (src, dst) in enumerate(
-        ((cache_hbm, cache), (wq_hbm, wq), (wk_hbm, wk), (wv_hbm, wv))
+        ((wq_hbm, wq), (cache_hbm, cache), (wk_hbm, wk), (wv_hbm, wv))
     ):
         c = pltpu.make_async_copy(src, dst, wsem.at[i])
         c.start()
@@ -82,9 +86,25 @@
         pl.semaphore_signal(barrier, inc=1, device_id=device, device_id_type=MESH)
     pl.semaphore_wait(barrier, len(partners))
 
+    count = owners.shape[0]
+    named = [owners[r] for r in range(count)]
+    keyed, coded = [], []
+    for r in range(count):
+        again = sum(((named[e] == named[r]).astype(jnp.int32) for e in range(r)), jnp.int32(0))
+        keyed.append(named[r] * 2 + again)
+        left = lengths[r // BPS] - (shard * BPS + r % BPS) * blk
+        coded.append(wanted[r] + 16 * jnp.minimum(jnp.maximum(left, 0), blk))
     lane = lax.broadcasted_iota(jnp.int32, (1, 128), 1)
     for p in range(slots):
-        ask_out[p] = jnp.where(lane == 0, tab[p, 0], jnp.where(lane == 1, tab[p, 3], 0))
+        owner = back(p)[0]
+        asking = []
+        for wave in range(2):
+            found = [jnp.where(keyed[r] == owner * 2 + wave, coded[r], 0) for r in range(count)]
+            one, two = sum(found[1:BPS], found[0]), sum(found[BPS + 1 :], found[BPS])
+            asking.append(one % 16 + two % 16)
+            tab[p, 3 * wave + 1] = one // 16
+            tab[p, 3 * wave + 2] = two // 16
+        ask_out[p] = jnp.where(lane == 0, asking[0], jnp.where(lane == 1, asking[1], 0))
     asks = []
     for p in range(1, slots):
         c = remote(ask_out.at[p], ask_in.at[p], asend.at[p], arecv.at[p], back(p))
@@ -101,12 +121,14 @@
         return c
 
     normed_tokens = rms_rows(tok_ref[...]).astype(BF16)
-    loads[1].wait()
+    loads[0].wait()
     q_all[pl.ds(pl.multiple_of(shard * rows, rows), rows), :] = silu(
         jnp.dot(normed_tokens, wq[...], preferred_element_type=F32)
     ).astype(BF16)
-    to_up = hop(0, q_rows(z, core), along(up, core))
-    to_down = hop(1, q_rows(z, core), along(down, core))
+    to_up = hop(0, q_rows(z, core, 0, half), along(up, core))
+    to_down = hop(1, q_rows(z, core, half, half), along(down, core))
+    to_up2 = hop(8, q_rows(z, core, half, half), along(up, core))
+    to_down2 = hop(9, q_rows(z, core, 0, half), along(down, core))
     to_side = hop(2, q_rows(z, core), along(z, 1 - core))
 
     for c in asks:
@@ -114,22 +136,27 @@
     c = pltpu.make_async_copy(ask_in, asked, wsem.at[6])
     c.start()
     c.wait()
-    loads[0].wait()
+    loads[1].wait()
     recv[0] = cache[asked[0, 0, 0]]
     landed[0] = cache[asked[0, 0, 1]]
     step = blk // PIECES
-    for wave in range(2):
-        for first, last in SETS[wave]:
+
+    def gather(wave, first, last):
+        for p in range(first, last):
+            stage[wave * slots + p] = cache[asked[p, 0, wave]]
+
+    def issue(wave, part):
+        first, last = SETS[part]
+        for piece in range(PIECES):
+            at = pl.ds(piece * step, step)
             for p in range(first, last):
-                stage[wave * slots + p] = cache[asked[p, 0, wave]]
-            for piece in range(PIECES):
-                part = pl.ds(piece * step, step)
-                for p in range(first, last):
-                    s = wave * slots + p
-                    remote(
-                        stage.at[s, part], recv.at[s, part], ssem.at[s], rsem.at[s], across(*OFFSETS[p])
-                    ).start()
-
+                s = wave * slots + p
+                remote(stage.at[s, at], recv.at[s, at], ssem.at[s], rsem.at[s], across(*OFFSETS[p])).start()
+
+    for part in range(len(SETS)):
+        gather(0, *SETS[part])
+        issue(0, part)
+    gather(1, 1, slots)
     blocks = width // blk
     for i, src in enumerate((wg_hbm, wo_hbm)):
         c = pltpu.make_async_copy(src, cache.at[pl.ds(i * blocks, blocks)], wsem.at[4 + i])
@@ -143,15 +170,31 @@
     def whole(s):
         return remote(stage.at[s], recv.at[s], ssem.at[s], rsem.at[s], along(z, 1 - core))
 
+    entry, places, codes = jnp.int32(slots // 2 - 1), [], []
+    for p in reversed(range(slots)):
+        n0, n1 = tab[p, 4], tab[p, 5]
+        real = n0 + n1 > 0
+        places.append(jnp.where(real, entry, -1))
+        codes.append(p + 16 * n0 + 4096 * n1)
+        entry = entry - real.astype(jnp.int32)
+    for e in range(slots // 2):
+        found = [jnp.where(places[i] == e, codes[i], 0) for i in range(slots)]
+        code = sum(found[1:], found[0])
+        late[e, 0] = code % 16
+        late[e, 1] = code // 16 % 256
+        late[e, 2] = code // 4096
+
     for i in range(usr_ref.shape[0]):
         line = jnp.broadcast_to(usr_ref[i : i + 1, :].astype(F32), (128, 128))
         umask[pl.ds(i * 128, 128), :] = line.T
 
     to_up.wait_recv()
     on_up = hop(3, q_rows(down, core, 0, half), along(up, core))
-    side_down = hop(4, q_rows(down, core), along(z, 1 - core))
     to_down.wait_recv()
     on_down = hop(5, q_rows(up, core, half, half), along(down, core))
+    to_up2.wait_recv()
+    side_down = hop(4, q_rows(down, core), along(z, 1 - core))
+    to_down2.wait_recv()
     side_up = hop(6, q_rows(up, core), along(z, 1 - core))
 
     def project(x, k, n0, n1):
@@ -172,8 +215,7 @@
     tile = 2 * rows
     scale = 0.5 / math.sqrt(head)
 
-    def attend_tile(zz, k, fresh=False):
-        at = pl.ds(pl.multiple_of(zz * tile, tile), tile)
+    def attend_rows(at, k):
         first_user = umask[at, :] == 0.0
         for h in range(HEADS):
             cols = slice(h * head, (h + 1) * head)
@@ -187,6 +229,11 @@
             )
             total[at, cols] += jnp.where(first_user, both[:, :head], both[:, head:])
 
+    def attend(k):
+        @pl.loop(0, total.shape[0] // TILE)
+        def _(t):
+            attend_rows(pl.ds(pl.multiple_of(t * TILE, TILE), TILE), k)
+
     def pair(buffer, base):
         return buffer[pl.ds(base, 2)].reshape(2 * blk, width)
 
@@ -216,20 +263,24 @@
     for c in (to_side, side_down, side_up, side_far):
         c.wait_recv()
 
+    def send_due(k):
+        for part, due in enumerate(DUE):
+
+            @pl.when(k == due)
+            def _():
+                issue(1, part)
+
     @pl.loop(0, PRE)
     def _(k):
-        @pl.loop(0, SIDE)
-        def _(zz):
-            attend_tile(zz, k)
+        send_due(k)
+        attend(k)
 
     @pl.loop(PRE, slots // 2)
     def _(k):
         arrive(2 * k)
         wave0_keys(k, 0)
-
-        @pl.loop(0, SIDE)
-        def _(zz):
-            attend_tile(zz, 0)
+        send_due(k)
+        attend(0)
 
     def land(p):
         arrive(slots + p)
@@ -250,9 +301,7 @@
         land(slots // 2 + 2 * k + 1)
         wave1_keys(k)
 
-        @pl.loop(0, SIDE)
-        def _(zz):
-            attend_tile(zz, 0)
+        attend(0)
 
     land(slots - 2)
     land(slots - 1)
@@ -260,7 +309,7 @@
 
     swaps = []
     for i, zz in enumerate((far, up, down, z)):
-        attend_tile(zz, 0)
+        attend_rows(pl.ds(pl.multiple_of(zz * tile, tile), tile), 0)
         for cc, dst in ((1 - core, give), (core, mine)):
             at = pl.ds(pl.multiple_of((zz * 2 + cc) * rows, rows), rows)
             sums = total[at, :]
@@ -304,7 +353,7 @@
     mixed = tok_ref[...].astype(F32) + jnp.dot(gated, late_weight(1), preferred_element_type=F32)
     out_ref[...] = mixed.astype(BF16)
 
-    for c in asks + [to_up, to_down, to_side, on_up, side_down, on_down, side_up, side_far] + swaps:
+    for c in asks + [to_up, to_down, to_up2, to_down2, to_side, on_up, side_down, on_down, side_up, side_far] + swaps:
         c.wait_send()
     for c in (s0, s1, s2, s3, s4, s5):
         c.wait_send()
@@ -329,37 +378,9 @@
     w_out,
 ):
     rows, width = cand_tokens.shape
-    grp = lax.axis_index("grp")
-    shard_id = lax.axis_index("hist")
-    owners = req_owner[0, 0, :, 0]
-    slots = req_slot[0, 0]
-    req_count = owners.shape[0]
     own_cache = hist_embed[:, 0]
     blk = own_cache.shape[1]
     positions = len(OFFSETS)
-
-    order = jnp.arange(req_count, dtype=jnp.int32)
-    before = (owners[None, :] == owners[:, None]) & (order[None, :] < order[:, None])
-    rank = jnp.sum(before.astype(jnp.int32), axis=1)
-    user = order // BPS
-    start = (shard_id * BPS + order % BPS) * blk
-    valid = jnp.clip(jnp.where(user == 0, hist_len[0], hist_len[1]) - start, 0, blk)
-    facts = jnp.stack([slots, jnp.where(user == 0, valid, 0), jnp.where(user == 1, valid, 0)])
-    dx = jnp.array([o[0] for o in OFFSETS], jnp.int32)
-    dy = jnp.array([o[1] for o in OFFSETS], jnp.int32)
-    owner_at = (grp // SIDE - dx + SIDE) % SIDE * SIDE + (grp % SIDE - dy + SIDE) % SIDE
-    chosen = (owners[None, None, :] == owner_at[:, None, None]) & (
-        rank[None, None, :] == jnp.arange(2, dtype=jnp.int32)[None, :, None]
-    )
-    tab = jnp.sum(jnp.where(chosen[:, :, None, :], facts[None, None], 0), axis=-1)
-    real = tab[:, 1, 1] + tab[:, 1, 2] > 0
-    place = jnp.arange(positions, dtype=jnp.int32)
-    behind = jnp.sum((real[None, :] & (place[None, :] > place[:, None])).astype(jnp.int32), axis=1)
-    entry = jnp.arange(positions // 2, dtype=jnp.int32)
-    hit = real[None, :] & (positions // 2 - 1 - behind[None, :] == entry[:, None])
-    found = jnp.stack([place, tab[:, 1, 1], tab[:, 1, 2]])
-    late = jnp.sum(jnp.where(hit[:, None, :], found[None], 0), axis=-1)
-
     smem = pl.BlockSpec(memory_space=pltpu.SMEM)
     vmem = pl.BlockSpec(memory_space=pltpu.VMEM)
     hbm = pl.BlockSpec(memory_space=pl.ANY)
@@ -370,7 +391,7 @@
     return pl.pallas_call(
         layer_kernel,
         out_shape=jax.ShapeDtypeStruct((rows, width), BF16),
-        in_specs=[smem, smem, vmem, vmem] + [hbm] * 6,
+        in_specs=[smem, smem, smem, vmem, vmem] + [hbm] * 6,
         out_specs=vmem,
         scratch_shapes=[
             pltpu.VMEM(own_cache.shape, BF16),
@@ -390,10 +411,12 @@
             pltpu.VMEM((3, rows, width), BF16),
             pltpu.VMEM((2, rows // 2, width), BF16),
             pltpu.VMEM((2, rows, width), BF16),
+            pltpu.SMEM((positions, 6), jnp.int32),
+            pltpu.SMEM((positions // 2, 3), jnp.int32),
             dma((7,)),
             dma((positions,)), dma((positions,)),
             dma((2 * positions,)), dma((2 * positions,)),
-            dma((8,)), dma((8,)),
+            dma((10,)), dma((10,)),
             dma((4,)), dma((4,)),
             dma((6,)), dma((6,)),
         ],
@@ -404,7 +427,7 @@
             flops=int(4e10), bytes_accessed=32 * 2**20, transcendentals=2**24
         ),
     )(
-        tab.reshape(positions, 6), late, cand_tokens, cand_user.reshape(group // 128, 128), own_cache,
+        req_owner.reshape(-1), req_slot.reshape(-1), hist_len, cand_tokens, cand_user.reshape(group // 128, 128), own_cache,
         w_query, w_key, w_value, w_gate.reshape(-1, blk, width), w_out.reshape(-1, blk, width),
     )
 

time: 182 us -> 149 us (0.82)
  Pallas kernels: 172 us -> 147 us
  other arithmetic: 4.83 us -> 0 us
  local copies, waits for them, and re-layouts: 4.64 us -> 1.87 us
    pallas_call x1, Pallas kernels: 172 us -> 147 us  [per_device(): pl.pallas_call(layer_kernel, out_shape=jax.ShapeDtypeStruct((rows, width)...]
where the time goes in v3:
time: 149 us
  Pallas kernels  147 us (99%)
  local copies, waits for them, and re-layouts  1.87 us (1%)
    pallas_call x1, Pallas kernels, per_device(): pl.pallas_call(layer_kernel, out_shape=jax.ShapeDtypeStruct((rows, width)...  147 us

profile of v3, /device:TPU:1, one launch (start us, length us, event | category | flops | bytes accessed | tf_op | source)
XLA Modules:
  0.0 148.5 jit_solution(18372515115415323449)
XLA Ops:
  0.0 146.6 %shard_map.109 = bf16[256,1024]{1,0:T(8,128)(2,1)} custom-call(s32[16]{0:T(128)} %bitcast.10, s32[16]{0:T(128)} %bitcast.11, s32[2]{0:T(128)} %lengths.1, bf16[256,1024]{1,0:T(8,128)(2,1)} %tok_ref.1, s32[16,128]{1,0:T(8,128)} %bitcast.9, bf16[16,128,1024]{2,1,0:T(8,128)(2,1)} %bitcast.6, bf16[1024,1024]{1,0:T(8,128)(2,1)} %wq_hbm.1, ...), custom_call_target="tpu_custom_call" | custom-call | flops 40000000000 | bytes 33554432 | tf_op jit(solution)/shard_map/pallas_call | solution.py:391
  146.6 1.9 %copy.13 = bf16[256,1024]{1,0:T(8,128)(2,1)} copy(bf16[256,1024]{1,0:T(8,128)(2,1)} %shard_map.109) | data formatting | bytes 1048576

commit v4 on v3

--- a/solution.py
+++ b/solution.py
@@ -27,7 +27,7 @@
 SETS = ((1, 9), (9, 12), (12, 15), (15, 16))
 PIECES = 4
 PRE = 4
-DUE = (0, 2, 4, 5)
+DUE = (0, 1, 3, 5)
 TILE = 2048
 
 
@@ -84,7 +84,6 @@
     partners = [across(*o) for o in OFFSETS[1:]] + [along(z, 1 - core), along(up, core), along(down, core)]
     for device in partners:
         pl.semaphore_signal(barrier, inc=1, device_id=device, device_id_type=MESH)
-    pl.semaphore_wait(barrier, len(partners))
 
     count = owners.shape[0]
     named = [owners[r] for r in range(count)]
@@ -105,6 +104,7 @@
             tab[p, 3 * wave + 1] = one // 16
             tab[p, 3 * wave + 2] = two // 16
         ask_out[p] = jnp.where(lane == 0, asking[0], jnp.where(lane == 1, asking[1], 0))
+    pl.semaphore_wait(barrier, len(partners))
     asks = []
     for p in range(1, slots):
         c = remote(ask_out.at[p], ask_in.at[p], asend.at[p], arecv.at[p], back(p))

time: 149 us -> 148 us (level)
  no operation moved by 1% of the time
where the time goes in v4:
time: 148 us
  Pallas kernels  146 us (99%)
  local copies, waits for them, and re-layouts  1.87 us (1%)
    pallas_call x1, Pallas kernels, per_device(): pl.pallas_call(layer_kernel, out_shape=jax.ShapeDtypeStruct((rows, width)...  146 us

profile of v4, /device:TPU:1, one launch (start us, length us, event | category | flops | bytes accessed | tf_op | source)
XLA Modules:
  0.0 147.5 jit_solution(11554229588332482211)
XLA Ops:
  0.0 145.6 %shard_map.109 = bf16[256,1024]{1,0:T(8,128)(2,1)} custom-call(s32[16]{0:T(128)} %bitcast.10, s32[16]{0:T(128)} %bitcast.11, s32[2]{0:T(128)} %lengths.1, bf16[256,1024]{1,0:T(8,128)(2,1)} %tok_ref.1, s32[16,128]{1,0:T(8,128)} %bitcast.9, bf16[16,128,1024]{2,1,0:T(8,128)(2,1)} %bitcast.6, bf16[1024,1024]{1,0:T(8,128)(2,1)} %wq_hbm.1, ...), custom_call_target="tpu_custom_call" | custom-call | flops 40000000000 | bytes 33554432 | tf_op jit(solution)/shard_map/pallas_call | solution.py:391
  145.6 1.9 %copy.13 = bf16[256,1024]{1,0:T(8,128)(2,1)} copy(bf16[256,1024]{1,0:T(8,128)(2,1)} %shard_map.109) | data formatting | bytes 1048576
